TPU v7x, 256 devices: a whole 4x4x8 slice. The times are simulated.
256 devices in a mesh: ctx: 32 (over z, y_hi, core), kvh: 8 (over y_lo, x).
Axes of the slice: x: 4, y: 4 (y_hi: 2, y_lo: 2; y = y_hi * 2 + y_lo), z: 8, core: 2. Of those that a mesh axis runs over, the one named last changes fastest.
Arguments:
- queries: bfloat16 [2, 4096, 5120], P(None, 'ctx', 'kvh'), may hold values from -140 to 140
- keys: bfloat16 [4096, 1024], P('ctx', 'kvh'), may hold values from -8 to 8
- values: bfloat16 [4096, 1024], P('ctx', 'kvh'), may hold values from -6 to 6
- grad_out: bfloat16 [2, 4096, 5120], P(None, 'ctx', 'kvh'), may hold values from -6 to 6
- query_weight: bfloat16 [2, 5120, 5120], P(None, 'ctx', 'kvh'), may hold values from -0.078125 to 0.078125
Outputs:
- input_grads: bfloat16 [2, 4096, 5120], P(None, 'ctx', 'kvh')
- grad_keys: bfloat16 [4096, 1024], P('ctx', 'kvh')
- grad_values: bfloat16 [4096, 1024], P('ctx', 'kvh')
All inputs are finite; a program needn't handle non-finite values.
Results may differ from a plain program's by a relative error of at most 0.0058.
Values may be sent and summed in bfloat16 or wider, within the bound.
A program may use at most 128 MiB of HBM per device.

v0:
```python
import math

import jax
import jax.numpy as jnp
from jax import lax
from jax.sharding import PartitionSpec as P

HEADS = 40
KV_HEADS = 8
HEAD_DIM = 128


lowest = -1e30


def head_rows(block, group_count):
    layers, tok_count, _ = block.shape
    repeat = HEADS // KV_HEADS
    shaped = block.reshape(layers, tok_count, group_count, repeat, HEAD_DIM)
    return shaped.transpose(2, 0, 3, 1, 4).reshape(
        group_count, layers * repeat * tok_count, HEAD_DIM
    )


def token_rows(block, layers, tok_count):
    group_count = block.shape[0]
    repeat = HEADS // KV_HEADS
    shaped = block.reshape(group_count, layers, repeat, tok_count, HEAD_DIM)
    return shaped.transpose(1, 3, 0, 2, 4).reshape(
        layers, tok_count, group_count * repeat * HEAD_DIM
    )


def head_major(block):
    return block.reshape(block.shape[0], -1, HEAD_DIM).transpose(1, 0, 2)


def over_keys(update, carry_state, key_part, value_part, unit_rows):
    extent = key_part.shape[1]
    block_len = math.gcd(extent, unit_rows)
    while block_len * 2 <= 512 and extent % (block_len * 2) == 0:
        block_len = block_len * 2

    def turn(counter, current):
        offset = counter * block_len
        key_block = lax.dynamic_slice_in_dim(key_part, offset, block_len, 1)
        value_block = lax.dynamic_slice_in_dim(value_part, offset, block_len, 1)
        return update(current, key_block, value_block, offset)

    return lax.fori_loop(0, extent // block_len, turn, carry_state)


def masked_scores(query, key_block, positions, key_first, scale_factor):
    raw_scores = (
        jnp.einsum("gmd,gpd->gmp", query, key_block, preferred_element_type=jnp.float32)
        * scale_factor
    )
    key_places = key_first + jnp.arange(key_block.shape[1], dtype=jnp.int32)
    visible = key_places[None, None, :] <= positions[None, :, None]
    return (raw_scores, visible)


def forward_tile(record, current, key_block, value_block, key_first, scale_factor):
    query, cotangent, positions, last_row = record

    def work(state_now):
        peak, total, weighted = state_now
        raw_scores, visible = masked_scores(query, key_block, positions, key_first, scale_factor)
        raw_scores = jnp.where(visible, raw_scores, lowest)
        new_peak = jnp.maximum(peak, jnp.max(raw_scores, axis=2))
        probs = jnp.where(visible, jnp.exp(raw_scores - new_peak[:, :, None]), 0.0)
        slopes = jnp.einsum(
            "gmd,gpd->gmp", cotangent, value_block, preferred_element_type=jnp.float32
        )
        factor = jnp.exp(peak - new_peak)
        return (
            new_peak,
            total * factor + jnp.sum(probs, axis=2),
            weighted * factor + jnp.sum(probs * slopes, axis=2),
        )

    return lax.cond(key_first <= last_row, work, lambda state_now: state_now, current)


def grad_tile(record, key_block, value_block, key_first, scale_factor):
    query, cotangent, positions, last_row, logsum, centre = record
    raw_scores, visible = masked_scores(query, key_block, positions, key_first, scale_factor)
    probs = jnp.where(visible, jnp.exp(raw_scores - logsum[:, :, None]), 0.0)
    slopes = jnp.einsum("gmd,gpd->gmp", cotangent, value_block, preferred_element_type=jnp.float32)
    mixed = (probs * (slopes - centre[:, :, None])).astype(jnp.bfloat16)
    results = []
    results.append(
        jnp.einsum("gmp,gpd->gmd", mixed, key_block, preferred_element_type=jnp.float32)
        * scale_factor
    )
    results.append(
        jnp.einsum("gmp,gmd->gpd", mixed, query, preferred_element_type=jnp.float32) * scale_factor
    )
    results.append(
        jnp.einsum(
            "gmp,gmd->gpd",
            probs.astype(jnp.bfloat16),
            cotangent,
            preferred_element_type=jnp.float32,
        )
    )
    return tuple(results)


def guarded_tile(record, key_block, value_block, key_first, scale_factor):
    group_count, row_count, _ = record[0].shape
    blanks = []
    blanks.append(jnp.zeros((group_count, row_count, HEAD_DIM), jnp.float32))
    blanks.append(jnp.zeros((group_count, key_block.shape[1], HEAD_DIM), jnp.float32))
    blanks.append(jnp.zeros((group_count, key_block.shape[1], HEAD_DIM), jnp.float32))
    blanks = tuple(blanks)
    return lax.cond(
        key_first <= record[3],
        lambda unused: grad_tile(record, key_block, value_block, key_first, scale_factor),
        lambda unused: blanks,
        0,
    )


def body(queries, keys, values, grad_out, query_weight):
    scale_factor = HEAD_DIM ** (-0.5)
    ctx_count = lax.axis_size("ctx")
    ctx_place = lax.axis_index("ctx")
    layers = queries.shape[0]
    tok_rows = queries.shape[1]
    group_count = keys.shape[1] // HEAD_DIM
    repeat = HEADS // KV_HEADS
    seg_pos = ctx_place * tok_rows + jnp.arange(tok_rows, dtype=jnp.int32)
    segments = [(queries, grad_out, seg_pos, ctx_place * tok_rows + tok_rows - 1)]
    bases = []
    seg_query, seg_grad, seg_pos, seg_last = segments[0]
    query = head_rows(seg_query, group_count)
    cotangent = head_rows(seg_grad, group_count)
    positions = jnp.tile(seg_pos, layers * repeat)
    bases.append((query, cotangent, positions, seg_last))
    forward_init = tuple(
        (
            (
                jnp.full(base[0].shape[:2], lowest, jnp.float32),
                jnp.zeros(base[0].shape[:2], jnp.float32),
                jnp.zeros(base[0].shape[:2], jnp.float32),
            )
            for base in bases
        )
    )
    pieces = (
        lax.all_gather(keys, "ctx", axis=0, tiled=True),
        lax.all_gather(values, "ctx", axis=0, tiled=True),
    )

    def update(current, key_block, value_block, block_first):
        return tuple(
            (
                forward_tile(base, state_now, key_block, value_block, block_first, scale_factor)
                for base, state_now in zip(bases, current)
            )
        )

    states = over_keys(update, forward_init, head_major(pieces[0]), head_major(pieces[1]), tok_rows)
    records = [
        base + (state_now[0] + jnp.log(state_now[1]), state_now[2] / state_now[1])
        for base, state_now in zip(bases, states)
    ]
    query_init = tuple((jnp.zeros(record[0].shape, jnp.float32) for record in records))
    total_rows = tok_rows * ctx_count
    start_state = (
        query_init,
        jnp.zeros((group_count, total_rows, HEAD_DIM), jnp.float32),
        jnp.zeros((group_count, total_rows, HEAD_DIM), jnp.float32),
    )
    pieces = (
        lax.all_gather(keys, "ctx", axis=0, tiled=True),
        lax.all_gather(values, "ctx", axis=0, tiled=True),
    )

    def update(current, key_block, value_block, block_first):
        query_sums, key_sums, value_sums = current
        new_sums = []
        block_len = key_block.shape[1]
        key_add = jnp.zeros((group_count, block_len, HEAD_DIM), jnp.float32)
        value_add = jnp.zeros((group_count, block_len, HEAD_DIM), jnp.float32)
        for record, query_acc in zip(records, query_sums):
            query_term, key_term, value_term = guarded_tile(
                record, key_block, value_block, block_first, scale_factor
            )
            new_sums.append(query_acc + query_term)
            key_add = key_add + key_term
            value_add = value_add + value_term
        key_sums = lax.dynamic_update_slice_in_dim(
            key_sums,
            lax.dynamic_slice_in_dim(key_sums, block_first, block_len, 1) + key_add,
            block_first,
            1,
        )
        value_sums = lax.dynamic_update_slice_in_dim(
            value_sums,
            lax.dynamic_slice_in_dim(value_sums, block_first, block_len, 1) + value_add,
            block_first,
            1,
        )
        return (tuple(new_sums), key_sums, value_sums)

    query_sums, key_sums, value_sums = over_keys(
        update, start_state, head_major(pieces[0]), head_major(pieces[1]), tok_rows
    )
    key_share, value_share = (
        lax.psum_scatter(key_sums, "ctx", scatter_dimension=1, tiled=True),
        lax.psum_scatter(value_sums, "ctx", scatter_dimension=1, tiled=True),
    )
    grad_keys = (
        key_share.transpose(1, 0, 2).reshape(tok_rows, group_count * HEAD_DIM).astype(jnp.bfloat16)
    )
    grad_values = (
        value_share.transpose(1, 0, 2)
        .reshape(tok_rows, group_count * HEAD_DIM)
        .astype(jnp.bfloat16)
    )
    query_grads = [
        token_rows(query_acc.astype(jnp.bfloat16), layers, seg[0].shape[1])
        for query_acc, seg in zip(query_sums, segments)
    ]
    joined = query_grads[0]
    terms = jnp.einsum(
        "lrh,lph->lrp",
        joined,
        lax.all_gather(query_weight, "ctx", axis=1, tiled=True),
        preferred_element_type=jnp.float32,
    )
    input_grads = lax.psum_scatter(terms, "kvh", scatter_dimension=2, tiled=True).astype(
        jnp.bfloat16
    )
    return (input_grads, grad_keys, grad_values)


def solution(mesh):
    in_specs = (
        P(None, "ctx", "kvh"),
        P("ctx", "kvh"),
        P("ctx", "kvh"),
        P(None, "ctx", "kvh"),
        P(None, "ctx", "kvh"),
    )
    out_specs = (P(None, "ctx", "kvh"), P("ctx", "kvh"), P("ctx", "kvh"))
    return jax.shard_map(body, mesh=mesh, in_specs=in_specs, out_specs=out_specs, check_vma=False)
```

profile of v0, /device:TPU:1, one launch (start us, length us, event | category | flops | bytes accessed | tf_op | source)
XLA Modules:
  0.0 625.6 jit_solution(16001713299944001)
XLA Ops:
  7.2 0.7 all-gather.4.cloned.1.call-update
  7.9 0.7 all-gather.6.cloned.1.call-update
  8.7 0.7 all-gather.8.cloned.1.call-update
  9.4 1.2 copy.14
  10.6 0.9 copy.15
  11.5 1.2 copy.16
  12.7 0.9 copy.17
  14.2 78.4 %all-gather.4.cloned.1.call-done = bf16[4096,128]{1,0:T(8,128)(2,1)} async-done(((bf16[128,128]{1,0:T(8,128)(2,1)}), bf16[4096,128]{1,0:T(8,128)(2,1)}) %all-gather.4.cloned.1.call-update) | async-done | bytes 1048592 | tf_op jit(solution)/shard_map/all_gather | solution.py:177
  92.6 77.2 %all-gather.6.cloned.1.call-done = bf16[4096,128]{1,0:T(8,128)(2,1)} async-done(((bf16[128,128]{1,0:T(8,128)(2,1)}), bf16[4096,128]{1,0:T(8,128)(2,1)}) %all-gather.6.cloned.1.call-update) | async-done | bytes 1048592 | tf_op jit(solution)/shard_map/all_gather | solution.py:178
  169.8 5.0 while.36
  169.8 4.7 conditional.6
  169.8 0.6 broadcast_bitcast_fusion
  170.4 1.6 fusion.44
  172.1 0.5 fusion.6
  172.6 1.8 fusion.7
  174.8 1.4 broadcast.106
  176.3 1.5 broadcast.106.clone
  177.8 45.7 %while.37 = (s32[]{:T(128)}, f32[1,1280,128]{2,1,0:T(8,128)}, f32[1,4096,128]{2,1,0:T(8,128)}, f32[1,4096,128]{2,1,0:T(8,128)}, s32[]{:T(128)}, /*index=5*/bf16[...) while((s32[]{:T(128)}, f32[1,1280,128]{2,1,0:T(8,128)}, ...), condition=%wide.region_10.11_spmd.clone, body=%wide.region_7.10_spmd.clone.sunk | while | flops 844792320 | bytes 18266952 | solution.py:50
  177.8 9.1 %conditional.7 = (f32[1,1280,128]{2,1,0:T(8,128)S(1)}, f32[1,512,128]{2,1,0:T(8,128)S(1)}, f32[1,512,128]{2,1,0:T(8,128)}) conditional(s32[]{:T(128)} %convert_element_type.62, () %tuple.107, (s32[]{:T(128)}, s32[128]{0:T(128)}, bf16[1,4096,128]{2,1,0:T(8,128)(2,1)}, s32[]{:T(128)}, bf16[1,1280,128]{2,1,0:T(8,128)(2,1)}, ...), branch_computations={%region_8.8_spmd, %region_9.9_spmd} | conditional | flops 844333568 | bytes 14727204 | solution.py:117
  177.8 0.6 broadcast_bitcast_fusion.1
  178.4 1.8 fusion.19
  180.2 1.6 fusion.22
  181.8 1.5 fusion.23
  183.2 1.5 fusion.29
  184.7 2.2 fusion.26
  186.9 2.0 add_dynamic-update-slice_fusion.3
  188.9 0.9 select_add_fusion.2
  189.8 0.8 conditional.7
  189.9 0.7 broadcast.98.clone
  190.6 2.0 add_dynamic-update-slice_fusion.3
  192.6 2.0 select_add_fusion.2
  194.6 0.8 conditional.7
  194.7 0.7 broadcast.98.clone
  195.4 2.0 add_dynamic-update-slice_fusion.3
  197.3 2.0 select_add_fusion.2
  199.4 0.8 conditional.7
  199.4 0.7 broadcast.98.clone
  200.2 2.0 add_dynamic-update-slice_fusion.3
  202.2 2.0 select_add_fusion.2
  204.2 0.8 conditional.7
  204.3 0.7 broadcast.98.clone
  205.0 2.0 add_dynamic-update-slice_fusion.3
  206.9 2.0 select_add_fusion.2
  208.9 0.8 conditional.7
  209.0 0.7 broadcast.98.clone
  209.7 2.0 add_dynamic-update-slice_fusion.3
  211.7 2.0 select_add_fusion.2
  213.7 0.8 conditional.7
  213.8 0.7 broadcast.98.clone
  214.5 2.0 add_dynamic-update-slice_fusion.3
  216.5 2.0 select_add_fusion.2
  218.5 0.8 conditional.7
  218.6 0.7 broadcast.98.clone
  219.3 2.0 add_dynamic-update-slice_fusion.3
  221.3 2.2 select_add_fusion.2
  223.6 0.5 reduce-scatter.6.cloned.1.call-update
  224.8 64.3 %all-gather.8.cloned.1.call-done = bf16[2,5120,640]{2,1,0:T(8,128)(2,1)} async-done(((bf16[2,160,640]{2,1,0:T(8,128)(2,1)}), bf16[2,5120,640]{2,1,0:T(8,128)(2,1)}) %all-gather.8.cloned.1.call-update) | async-done | bytes 13107216 | tf_op jit(solution)/shard_map/all_gather | solution.py:231
  289.1 11.4 %fusion.46 = f32[2,128,5120]{2,1,0:T(8,128)} fusion(bf16[2,128,640]{1,2,0:T(8,128)(2,1)S(1)} %bitcast.86, bf16[2,5120,640]{2,1,0:T(8,128)(2,1)} %all-gather.8.cloned.1.call-done), kind=kOutput, calls=%fused_computation.65 | convolution fusion | flops 1677721600 | bytes 18677760 | tf_op jit(solution)/shard_map/lrh,lph->lrp/dot_general | solution.py:228
  300.6 123.4 %reduce-scatter.8.cloned.1.call-done = f32[1,128,128]{2,1,0:T(8,128)} async-done(((f32[1,4096,128]{2,1,0:T(8,128)}), f32[1,128,128]{2,1,0:T(8,128)}) %reduce-scatter.8.cloned.1.call-update) | async-done | bytes 65552 | tf_op jit(solution)/shard_map/reduce_scatter | solution.py:213
  424.0 1.5 convert_bitcast_fusion
  425.4 120.4 %reduce-scatter.6.cloned.1.call-done = f32[1,128,128]{2,1,0:T(8,128)} async-done(((f32[1,4096,128]{2,1,0:T(8,128)}), f32[1,128,128]{2,1,0:T(8,128)}) %reduce-scatter.6.cloned.1.call-update) | async-done | bytes 65552 | tf_op jit(solution)/shard_map/reduce_scatter | solution.py:212
  545.8 1.5 convert_bitcast_fusion.1
  547.2 69.7 %reduce-scatter.4.cloned.1.call-done = f32[2,128,640]{2,1,0:T(8,128)} async-done(((f32[2,128,5120]{2,1,0:T(8,128)}), f32[2,128,640]{2,1,0:T(8,128)}) %reduce-scatter.4.cloned.1.call-update) | async-done | bytes 655376 | tf_op jit(solution)/shard_map/reduce_scatter | solution.py:234
  616.9 1.8 convert_element_type.45
  (46 shorter events, 2.1 us)
Async XLA Ops:
  7.2 85.4 %all-gather.4.cloned.1.call-start = ((), (), s32[]{:S(2)}) async-start(), calls=%async_computation.3 | async-start | bytes 1081344 | tf_op jit(solution)/shard_map/all_gather | solution.py:177
  7.9 161.9 %all-gather.6.cloned.1.call-start = ((), (), s32[]{:S(2)}) async-start(), calls=%async_computation.4 | async-start | bytes 1081344 | tf_op jit(solution)/shard_map/all_gather | solution.py:178
  8.6 280.5 %all-gather.8.cloned.1.call-start = ((), (), s32[]{:S(2)}) async-start(), calls=%async_computation.5 | async-start | bytes 13516800 | tf_op jit(solution)/shard_map/all_gather | solution.py:231
  9.4 414.6 %reduce-scatter.8.cloned.1.call-start = ((), (), s32[]{:S(2)}) async-start(), calls=%async_computation.8 | async-start | bytes 2162688 | tf_op jit(solution)/shard_map/reduce_scatter | solution.py:213
  223.5 1.1 copy-start
  223.5 322.3 %reduce-scatter.6.cloned.1.call-start = ((), (), s32[]{:S(2)}) async-start(), calls=%async_computation.7 | async-start | bytes 2162688 | tf_op jit(solution)/shard_map/reduce_scatter | solution.py:212
  224.1 392.8 %reduce-scatter.4.cloned.1.call-start = ((), (), s32[]{:S(2)}) async-start(), calls=%async_computation.6 | async-start | bytes 5898240 | tf_op jit(solution)/shard_map/reduce_scatter | solution.py:234
Sparse Core Ops, SparseCore 0:
  10.8 81.7 all-gather.3
  95.4 74.3 all-gather.5
  172.6 116.4 all-gather.7
  293.1 130.8 reduce-scatter.7
  428.5 117.2 reduce-scatter.5
  548.2 68.6 reduce-scatter.3
where the time goes:
time: 628 us; the launch traced here: 626 us
  waiting for transfers between devices  536 us (85%)
  other arithmetic  37 us (6%)
  matrix products  23.3 us (4%)
  local copies, waits for them, and re-layouts  14.5 us (2%)
  between operations  14.2 us (2%)
    reduce_scatter x1, waiting for transfers between devices, body(): lax.psum_scatter(value_sums, 'ctx', scatter_dimension=1, tiled=True)  123 us
    reduce_scatter x1, waiting for transfers between devices, body(): lax.psum_scatter(key_sums, 'ctx', scatter_dimension=1, tiled=True)  120 us
    all_gather x1, waiting for transfers between devices, body(): lax.all_gather(keys, 'ctx', axis=0, tiled=True)  78.4 us
    all_gather x1, waiting for transfers between devices, body(): lax.all_gather(values, 'ctx', axis=0, tiled=True)  77.2 us
    reduce_scatter x1, waiting for transfers between devices, body(): lax.psum_scatter(terms, 'kvh', scatter_dimension=2, tiled=True)  69.7 us
    all_gather x1, waiting for transfers between devices, body(): lax.all_gather(query_weight, 'ctx', axis=1, tiled=True)  64.3 us
    dynamic_update_slice x8, other arithmetic, update(): lax.dynamic_update_slice_in_dim(value_sums, lax.dynamic_slice_in_dim(valu...  15.8 us
    add x8, other arithmetic, update(): new_sums.append(query_acc + query_term)  15.2 us
  transfers between devices with their start and end apart: 6, of which 6 were waited for; matrix products, arithmetic and copies ran while one was open for 12% of the time, Pallas kernels for 0%

commit v1 on v0

v1 whole, which is shorter than its diff:
```python
import jax
import jax.numpy as jnp
from jax import lax
from jax.experimental import pallas as pl
from jax.experimental.pallas import tpu as pltpu
from jax.sharding import PartitionSpec as P

SCALE = 128 ** -0.5
LOG2 = SCALE * 1.4426950408889634
LOWEST = -1e30
NT = (((1,), (1,)), ((), ()))
MESH = pl.DeviceIdType.MESH
BF = jnp.bfloat16
F32 = jnp.float32
BLOCK = 2048
SUB = 128
PARTS = BLOCK // SUB
PAIRS = 5
POLLS = 14


def dot_nt(a, b):
    return lax.dot_general(a, b, NT, preferred_element_type=F32)


def dot(a, b):
    return jnp.dot(a, b, preferred_element_type=F32)


def send(src, dst, send_sem, recv_sem, device):
    return pltpu.make_async_remote_copy(
        src_ref=src,
        dst_ref=dst,
        send_sem=send_sem,
        recv_sem=recv_sem,
        device_id=device,
        device_id_type=MESH,
    )


def kernel(
    q_ref, k_ref, v_ref, do_ref, w_ref,
    out_ref, gk_ref, gv_ref,
    kv, kt, e_ref, d_ref, peaks, qs, dos, dkv, w_all, a_all, ct, xr, fs, fr,
    sb, sbr, yb, ybr, zb, zr,
    kv_y, kv_rs, kv_rr, kv_ls, kv_lr, kv_ss, kv_sr,
    w_y, w_rs, w_rr, w_ls, w_lr, w_ss, w_sr,
    a_s, a_r, x_s, x_r, f_s, f_r,
    s_s, s_r, y_s, y_r, z_s, z_r,
):
    i = lax.axis_index("ctx")
    j = lax.axis_index("kvh")
    z = lax.div(i, 4)
    r = lax.rem(i, 4)
    yh = lax.div(r, 2)
    c = lax.rem(i, 2)
    yl = lax.div(j, 4)
    x = lax.rem(j, 4)

    def ring(a):
        return lax.rem(a + 8, 8)

    sibling = {"ctx": i + 1 - 2 * c, "kvh": j}
    right = {"ctx": ring(z + 1) * 4 + r, "kvh": j}
    left = {"ctx": ring(z - 1) * 4 + r, "kvh": j}
    flip_i = i + 2 - 4 * yh
    flip_j = j + 4 - 8 * yl
    y_peers = [{"ctx": flip_i, "kvh": j}, {"ctx": i, "kvh": flip_j}, {"ctx": flip_i, "kvh": flip_j}]
    y_places = [(1 - yh, yl), (yh, 1 - yl), (1 - yh, 1 - yl)]
    x_places = [lax.rem(x + t, 4) for t in (1, 2, 3)]
    x_peers = [{"ctx": i, "kvh": yl * 4 + p} for p in x_places]

    barrier = pltpu.get_barrier_semaphore()
    for peer in [sibling] + y_peers + x_peers:
        pl.semaphore_signal(barrier, inc=1, device_id=peer, device_id_type=MESH)
    for t in range(1, 8):
        pl.semaphore_signal(
            barrier, inc=1, device_id={"ctx": ring(z + t) * 4 + r, "kvh": j}, device_id_type=MESH
        )
    pl.semaphore_wait(barrier, 14)

    kv[0, z, yh, c] = k_ref[...]
    kv[1, z, yh, c] = v_ref[...]
    own = kv.at[:, z, yh, c]
    kv_far = send(own, own, kv_y.at[0], kv_y.at[1], y_peers[0])
    kv_far.start()
    sib_sends = []

    def to_sibling(ref):
        n = len(sib_sends)
        copy = send(ref, ref, kv_ss.at[n], kv_sr.at[n], sibling)
        copy.start()
        sib_sends.append(copy)

    to_sibling(own)
    w_swap = send(
        w_ref.at[:, pl.ds(pl.multiple_of((1 - yl) * 80, 16), 80), :],
        w_all.at[:, yl, z, c],
        w_y.at[0],
        w_y.at[1],
        y_peers[1],
    )
    w_swap.start()
    w_all[:, yl, z, c] = w_ref[:, pl.ds(pl.multiple_of(yl * 80, 16), 80), :]
    kv_far.wait_recv()
    block = kv.at[:, z, :, c]
    rights = [send(block, block, kv_rs.at[0], kv_rr.at[0], right)]
    lefts = [send(block, block, kv_ls.at[0], kv_lr.at[0], left)]
    rights[0].start()
    lefts[0].start()
    to_sibling(kv.at[:, z, 1 - yh, c])
    dkv[...] = jnp.zeros_like(dkv)
    for s in range(4):
        for sends, toward, ss, rs, sign, half in (
            (rights, right, kv_rs, kv_rr, -1, 0),
            (lefts, left, kv_ls, kv_lr, 1, 1),
        ):
            sends[s].wait_recv()
            zz = ring(z + sign * (s + 1))
            block = kv.at[:, zz, :, c] if s < 3 else kv.at[half, zz, :, c]
            if s < 3:
                onward = block if s < 2 else kv.at[half, zz, :, c]
                copy = send(onward, onward, ss.at[s + 1], rs.at[s + 1], toward)
                copy.start()
                sends.append(copy)
            to_sibling(block)

    def w_part(layer, half, zz):
        return w_all.at[layer, half, zz, c]

    def w_send(layer, half, zz, n):
        ref = w_part(layer, half, zz)
        if layer == 0:
            return send(ref, ref, w_rs.at[n], w_rr.at[n], right)
        return send(ref, ref, w_ls.at[n], w_lr.at[n], left)

    def w_sib(layer, half, zz, n):
        ref = w_part(layer, half, zz)
        return send(ref, ref, w_ss.at[layer, n], w_sr.at[layer, n], sibling)

    w_swap.wait_recv()
    for half in range(2):
        for layer in range(2):
            w_send(layer, half, z, half).start()
    for half in range(2):
        for layer in range(2):
            w_sib(layer, half, z, half).start()

    def poll(n):
        step = lax.div(n, 2)
        half = lax.rem(n, 2)
        for layer, sign in ((0, -1), (1, 1)):
            zz = ring(z + sign * (step + 1))
            w_send(layer, half, zz, n).wait_recv()

            @pl.when(step < 6)
            def _():
                w_send(layer, half, zz, n + 2).start()

            w_sib(layer, half, zz, n + 2).start()

    for copy in sib_sends:
        copy.wait_recv()

    for b in range(8):
        whole = kv[0, b].reshape(512, 128).astype(F32)
        kt[b // 4, :, (b % 4) * 512 : (b % 4 + 1) * 512] = whole.T.astype(BF)

    last = lax.div(z, 4)
    lane = lax.broadcasted_iota(jnp.int32, (SUB, 256), 1)
    place = z * 512 + r * 128 + lax.rem(lane, 128)

    def pair(h, carry):
        column = pl.ds(pl.multiple_of(h * 128, 128), 128)
        for layer in range(2):
            rows = slice(layer * 128, (layer + 1) * 128)
            qs[rows] = q_ref[layer, :, column]
            dos[rows] = do_ref[layer, :, column]
        query = qs[...]
        cotangent = dos[...]

        def forward(b, state, masked=False):
            m, total, weighted = state
            for n in range(PARTS):
                rows = pl.ds(n * SUB, SUB)
                zz = 4 * b + n // 4
                s = dot_nt(kv[0, zz, n // 2 % 2, n % 2], query)
                if masked:
                    key_place = lax.broadcasted_iota(jnp.int32, (SUB, 256), 0) + (b * BLOCK + n * SUB)
                    s = jnp.where(key_place <= place, s, LOWEST)
                d = dot_nt(kv[1, zz, n // 2 % 2, n % 2], cotangent)
                s = s.reshape(SUB // 8, 8, 256)
                peak = jnp.max(s, axis=0)
                e = jnp.exp2((s - peak[None]) * LOG2)
                part_total = jnp.sum(e, axis=0)
                part_weighted = jnp.sum(e * d.reshape(SUB // 8, 8, 256), axis=0)
                e_ref[b, rows] = e.reshape(SUB, 256)
                d_ref[b, rows] = d
                peaks[b, n] = peak
                new = jnp.maximum(m, peak)
                f0 = jnp.exp2((m - new) * LOG2)
                f1 = jnp.exp2((peak - new) * LOG2)
                total = total * f0 + part_total * f1
                weighted = weighted * f0 + part_weighted * f1
                m = new
            return m, total, weighted

        zero = jnp.zeros((8, 256), F32)
        state = lax.fori_loop(0, last, forward, (jnp.full((8, 256), LOWEST, F32), zero, zero))
        m8, total8, weighted8 = forward(last, state, True)
        poll(2 * h)
        m = jnp.max(m8, axis=0, keepdims=True)
        f = jnp.exp2((m8 - m) * LOG2)
        inverse = 1.0 / jnp.sum(total8 * f, axis=0, keepdims=True)
        delta = jnp.sum(weighted8 * f, axis=0, keepdims=True) * inverse

        def backward(b, dq):
            probs = []
            mixed = []
            for n in range(PARTS):
                rows = pl.ds(n * SUB, SUB)
                f = jnp.exp2((peaks[b, n] - m) * LOG2) * inverse
                p = (e_ref[b, rows].reshape(SUB // 8, 8, 256) * f[None]).reshape(SUB, 256)
                mixed.append((p * (d_ref[b, rows] - delta)).astype(BF))
                probs.append(p.astype(BF))
            probs = jnp.concatenate(probs, 0)
            mixed = jnp.concatenate(mixed, 0)
            here = pl.ds(4 * b, 4)
            shape = (4, 2, 2, 128, 128)
            dkv[1, here] += dot(probs, cotangent).reshape(shape)
            dkv[0, here] += dot(mixed, query).reshape(shape)
            return dq + dot(kt[b], mixed)

        dq = lax.fori_loop(0, last + 1, backward, jnp.zeros((128, 256), F32))
        for layer in range(2):
            a_all[h, layer, yl, yh] = (dq[:, layer * 128 : (layer + 1) * 128].T * SCALE).astype(BF)
        ref = a_all.at[h, :, yl, yh]
        for t in range(3):
            send(ref, ref, a_s.at[h, t], a_r.at[h, t], y_peers[t]).start()
        poll(2 * h + 1)
        return carry

    lax.fori_loop(0, PAIRS, pair, 0)

    def stage_sibling(zz, carry):
        sb[0, zz] = (dkv[0, zz, :, 1 - c] * SCALE).astype(BF)
        sb[1, zz] = dkv[1, zz, :, 1 - c].astype(BF)
        send(sb.at[:, zz], sbr.at[:, zz], s_s.at[zz], s_r.at[zz], sibling).start()
        return carry

    lax.fori_loop(0, z + 1, stage_sibling, 0)

    def late(n, carry):
        poll(n)
        return carry

    lax.fori_loop(2 * PAIRS, POLLS, late, 0)

    def stage_y(zz, carry):
        copy = send(sb.at[:, zz], sbr.at[:, zz], s_s.at[zz], s_r.at[zz], sibling)
        copy.wait_recv()
        for n, scale in ((0, SCALE), (1, 1.0)):
            far = dkv[n, zz, 1 - yh, c] * scale + sbr[n, zz, 1 - yh].astype(F32)
            yb[n, zz] = far.astype(BF)
        send(yb.at[:, zz], ybr.at[:, zz], y_s.at[zz], y_r.at[zz], y_peers[0]).start()
        for n, scale in ((0, SCALE), (1, 1.0)):
            dkv[n, zz, yh, c] = dkv[n, zz, yh, c] * scale + sbr[n, zz, yh].astype(F32)
        return carry

    lax.fori_loop(0, z + 1, stage_y, 0)

    for h in range(PAIRS):
        for t, (ph, pw) in enumerate(y_places):
            ref = a_all.at[h, :, pw, ph]
            send(ref, ref, a_s.at[h, t], a_r.at[h, t], y_peers[t]).wait_recv()
    for layer in range(2):
        for n in range(16):
            zz = ring(z - n // 2) if layer == 0 else ring(z + n // 2)
            w_sib(layer, n % 2, zz, n).wait_recv()
    x_sends = []
    for layer in range(2):
        sides = [
            jnp.concatenate([a_all[h, layer, w].reshape(256, 128) for h in range(PAIRS)], axis=1)
            for w in range(2)
        ]
        for hi in range(2):
            total = dot_nt(w_all[layer, 0, 4 * hi : 4 * hi + 4].reshape(640, 640), sides[0])
            total = total + dot_nt(w_all[layer, 1, 4 * hi : 4 * hi + 4].reshape(640, 640), sides[1])
            ct[layer, hi] = total.astype(BF).reshape(4, 2, 80, 256)
        for t in range(3):
            copy = send(
                ct.at[layer, :, x_places[t]], xr.at[t, layer], x_s.at[layer, t], x_r.at[layer, t], x_peers[t]
            )
            copy.start()
            x_sends.append(copy)

    def stage_z(zz, carry):
        send(yb.at[:, zz], ybr.at[:, zz], y_s.at[zz], y_r.at[zz], y_peers[0]).wait_recv()
        for n in range(2):
            near = dkv[n, zz, yh, c] + ybr[n, zz].astype(F32)
            dkv[n, zz, yh, c] = near
            zb[n, zz] = near.astype(BF)

        @pl.when(zz < z)
        def _():
            send(
                zb.at[:, zz], zr.at[:, z], z_s.at[zz], z_r.at[z], {"ctx": zz * 4 + r, "kvh": j}
            ).start()

        return carry

    lax.fori_loop(0, z + 1, stage_z, 0)

    f_sends = []
    for layer in range(2):
        for t in range(3):
            x_sends[layer * 3 + t].wait_recv()
        total = ct[layer, :, x].astype(F32)
        for t in range(3):
            total = total + xr[t, layer].astype(F32)
        total = total.astype(BF)
        for half in range(2):
            fs[half, :, layer] = total[..., half * 128 : (half + 1) * 128]
        for t, (ph, pw) in enumerate(y_places):
            copy = send(
                fs.at[ph, pw, layer], fr.at[layer, yh, :, yl], f_s.at[layer, t], f_r.at[layer, t], y_peers[t]
            )
            copy.start()
            f_sends.append(copy)
        fr[layer, yh, :, yl] = fs[yh, yl, layer]

    def gather_z(zz, carry):
        send(zb.at[:, z], zr.at[:, zz], z_s.at[z], z_r.at[zz], left).wait_recv()
        for n in range(2):
            dkv[n, z, yh, c] += zr[n, zz].astype(F32)
        return carry

    lax.fori_loop(z + 1, 8, gather_z, 0)
    gk_ref[...] = dkv[0, z, yh, c].astype(BF)
    gv_ref[...] = dkv[1, z, yh, c].astype(BF)

    for layer in range(2):
        for t in range(3):
            f_sends[layer * 3 + t].wait_recv()
        out_ref[layer] = fr[layer].reshape(640, 128).astype(F32).T.astype(BF)

    for copy in [kv_far, w_swap] + sib_sends + rights + lefts + x_sends + f_sends:
        copy.wait_send()
    for n in range(POLLS):
        for layer in range(2):
            w_send(layer, 0, z, n).wait_send()
    for n in range(POLLS + 2):
        for layer in range(2):
            w_sib(layer, 0, z, n).wait_send()
    for h in range(PAIRS):
        for t in range(3):
            ref = a_all.at[h, :, yl, yh]
            send(ref, ref, a_s.at[h, t], a_r.at[h, t], y_peers[t]).wait_send()

    def drain(zz, carry):
        send(sb.at[:, zz], sbr.at[:, zz], s_s.at[zz], s_r.at[zz], sibling).wait_send()
        send(yb.at[:, zz], ybr.at[:, zz], y_s.at[zz], y_r.at[zz], y_peers[0]).wait_send()

        @pl.when(zz < z)
        def _():
            send(zb.at[:, zz], zr.at[:, z], z_s.at[zz], z_r.at[z], left).wait_send()

        return carry

    lax.fori_loop(0, z + 1, drain, 0)


def body(queries, keys, values, grad_out, query_weight):
    dma = pltpu.SemaphoreType.DMA
    vmem = pltpu.VMEM
    return pl.pallas_call(
        kernel,
        out_shape=(
            jax.ShapeDtypeStruct((2, 128, 640), BF),
            jax.ShapeDtypeStruct((128, 128), BF),
            jax.ShapeDtypeStruct((128, 128), BF),
        ),
        in_specs=[pl.BlockSpec(memory_space=pltpu.VMEM)] * 5,
        out_specs=[pl.BlockSpec(memory_space=pltpu.VMEM)] * 3,
        scratch_shapes=[
            vmem((2, 8, 2, 2, 128, 128), BF),
            vmem((2, 128, BLOCK), BF),
            vmem((2, BLOCK, 256), F32),
            vmem((2, BLOCK, 256), F32),
            vmem((2, PARTS, 8, 256), F32),
            vmem((256, 128), BF),
            vmem((256, 128), BF),
            vmem((2, 8, 2, 2, 128, 128), F32),
            vmem((2, 2, 8, 2, 80, 640), BF),
            vmem((PAIRS, 2, 2, 2, 128, 128), BF),
            vmem((2, 2, 4, 2, 80, 256), BF),
            vmem((3, 2, 2, 2, 80, 256), BF),
            vmem((2, 2, 2, 2, 80, 128), BF),
            vmem((2, 2, 2, 2, 80, 128), BF),
            vmem((2, 8, 2, 128, 128), BF),
            vmem((2, 8, 2, 128, 128), BF),
            vmem((2, 8, 128, 128), BF),
            vmem((2, 8, 128, 128), BF),
            vmem((2, 8, 128, 128), BF),
            vmem((2, 8, 128, 128), BF),
            dma((2,)), dma((4,)), dma((4,)), dma((4,)), dma((4,)), dma((10,)), dma((10,)),
            dma((2,)), dma((POLLS,)), dma((POLLS,)), dma((POLLS,)), dma((POLLS,)),
            dma((2, POLLS + 2)), dma((2, POLLS + 2)),
            dma((PAIRS, 3)), dma((PAIRS, 3)), dma((2, 3)), dma((2, 3)), dma((2, 3)), dma((2, 3)),
            dma((8,)), dma((8,)), dma((8,)), dma((8,)), dma((8,)), dma((8,)),
        ],
        compiler_params=pltpu.CompilerParams(
            collective_id=0, has_side_effects=True, vmem_limit_bytes=56 << 20
        ),
    )(queries, keys, values, grad_out, query_weight)


def solution(mesh):
    cols = P(None, "ctx", "kvh")
    flat = P("ctx", "kvh")
    return jax.shard_map(
        body,
        mesh=mesh,
        in_specs=(cols, flat, flat, cols, cols),
        out_specs=(cols, flat, flat),
        check_vma=False,
    )
```

time: 628 us -> 98.4 us (0.16)
  waiting for transfers between devices: 536 us -> 0 us
  Pallas kernels: 0 us -> 94.5 us
  other arithmetic: 37 us -> 0 us
  matrix products: 23.3 us -> 0 us
  between operations: 14.2 us -> 0.65 us
  local copies, waits for them, and re-layouts: 14.5 us -> 3.12 us
    reduce_scatter x3 -> x0, waiting for transfers between devices: 313 us -> none  [the longest x1 123 us: body(): lax.psum_scatter(value_sums, 'ctx', scatter_dimension=1, tiled=True)]
    all_gather x3 -> x0, waiting for transfers between devices: 220 us -> none  [the longest x1 78.4 us: body(): lax.all_gather(keys, 'ctx', axis=0, tiled=True)]
    pallas_call x0 -> x1, Pallas kernels: none -> 94.5 us  [body(): pl.pallas_call(kernel, out_shape=(jax.ShapeDtypeStruct((2, 128, 640), BF)...]
    dot_general x8 -> x0, matrix products: 23.3 us -> none  [the longest x1 11.4 us: body(): jnp.einsum('lrh,lph->lrp', joined, lax.all_gather(query_weight, 'ctx', ax...]
    add x12 -> x0, other arithmetic: 15.8 us -> none  [the longest x8 15.2 us: update(): new_sums.append(query_acc + query_term)]
    dynamic_update_slice x8 -> x0, other arithmetic: 15.8 us -> none  [update(): lax.dynamic_update_slice_in_dim(value_sums, lax.dynamic_slice_in_dim(valu...]
    another operation x25 -> x0, local copies, waits for them, and re-layouts: 8.44 us -> none
  transfers between devices with their start and end apart: 6 -> 0, of which waited for: 6 -> 0; matrix products, arithmetic and copies ran while one was open for 12% -> 0% of each run, Pallas kernels for 0% -> 0%
where the time goes in v1:
time: 98.4 us; the launch traced here: 98.3 us
  Pallas kernels  94.5 us (96%)
  local copies, waits for them, and re-layouts  3.12 us (3%)
    pallas_call x1, Pallas kernels, body(): pl.pallas_call(kernel, out_shape=(jax.ShapeDtypeStruct((2, 128, 640), BF)...  94.5 us
    unnamed x7, local copies, waits for them, and re-layouts  3.12 us

profile of v1, /device:TPU:1, one launch (start us, length us, event | category | flops | bytes accessed | tf_op | source)
XLA Modules:
  0.0 98.3 jit_solution(16451339954039864757)
XLA Ops:
  0.6 94.5 %shard_map.76 = (bf16[2,128,640]{2,1,0:T(8,128)(2,1)}, bf16[128,128]{1,0:T(8,128)(2,1)}, bf16[128,128]{1,0:T(8,128)(2,1)}) custom-call(bf16[2,128,640]{2,1,0:T(8,128)(2,1)} %q_ref.1, bf16[128,128]{1,0:T(8,128)(2,1)} %k_ref.1, bf16[128,128]{1,0:T(8,128)(2,1)} %v_ref.1, bf16[2,128,640]{2,1,0:T(8,128)(2,1)} %do_ref.1, bf16[2,160,640]{2,1,0:T(8,128)(2,1)} %w_ref.1), custom_call_target="tpu_custom_call" | custom-call | tf_op jit(solution)/shard_map/pallas_call | solution.py:376
  95.1 0.0 copy-start.1
  95.1 1.7 %copy.11 = bf16[2,128,640]{2,1,0:T(8,128)(2,1)} copy(bf16[2,128,640]{2,1,0:T(8,128)(2,1)} %get-tuple-element.6) | data formatting | bytes 655360
  96.9 0.0 copy-done.1
  96.9 0.0 copy-start
  96.9 0.6 copy.12
  97.5 0.2 copy-done
  97.6 0.6 copy.13
Async XLA Ops:
  95.1 1.7 %copy-start.1 = (bf16[128,128]{1,0:T(8,128)(2,1)S(1)}, bf16[128,128]{1,0:T(8,128)(2,1)}, u32[]{:S(2)}) copy-start(bf16[128,128]{1,0:T(8,128)(2,1)} %get-tuple-element.7) | copy-start | bytes 98308
  96.9 0.8 copy-start

commit v2 on v1

v2 whole, which is shorter than its diff:
```python
import jax
import jax.numpy as jnp
from jax import lax
from jax.experimental import pallas as pl
from jax.experimental.pallas import tpu as pltpu
from jax.sharding import PartitionSpec as P

SCALE = 128 ** -0.5
LOG2 = SCALE * 1.4426950408889634
LOWEST = -1e30
NT = (((1,), (1,)), ((), ()))
MESH = pl.DeviceIdType.MESH
BF = jnp.bfloat16
F32 = jnp.float32
BLOCK = 2048
SUB = 128
PARTS = BLOCK // SUB
PAIRS = 5


def dot_nt(a, b):
    return lax.dot_general(a, b, NT, preferred_element_type=F32)


def dot(a, b):
    return jnp.dot(a, b, preferred_element_type=F32)


def send(src, dst, send_sem, recv_sem, device):
    return pltpu.make_async_remote_copy(
        src_ref=src,
        dst_ref=dst,
        send_sem=send_sem,
        recv_sem=recv_sem,
        device_id=device,
        device_id_type=MESH,
    )


def kernel(
    q_ref, k_ref, v_ref, do_ref, w_ref,
    out_ref, gk_ref, gv_ref,
    kv, kt, e_ref, d_ref, peaks, qs, dos, dkv, w_all, a_all, ct, xr, fs, fr,
    sb, sbr, yb, ybr, zb, zr,
    kv_s, kv_r, ky_s, ky_r, kc_s, kc_r,
    ws_s, ws_r, w_s, w_r, wc_s, wc_r,
    a_s, a_r, x_s, x_r, f_s, f_r,
    s_s, s_r, y_s, y_r, z_s, z_r,
):
    i = lax.axis_index("ctx")
    j = lax.axis_index("kvh")
    z = lax.div(i, 4)
    r = lax.rem(i, 4)
    yh = lax.div(r, 2)
    c = lax.rem(i, 2)
    yl = lax.div(j, 4)
    x = lax.rem(j, 4)

    def ring(a):
        return lax.rem(a + 8, 8)

    sibling = {"ctx": i + 1 - 2 * c, "kvh": j}
    sides = [{"ctx": ring(z + 1) * 4 + r, "kvh": j}, {"ctx": ring(z - 1) * 4 + r, "kvh": j}]
    flip_i = i + 2 - 4 * yh
    flip_j = j + 4 - 8 * yl
    y_peers = [{"ctx": flip_i, "kvh": j}, {"ctx": i, "kvh": flip_j}, {"ctx": flip_i, "kvh": flip_j}]
    y_places = [(1 - yh, yl), (yh, 1 - yl), (1 - yh, 1 - yl)]
    x_places = [lax.rem(x + t, 4) for t in (1, 2, 3)]
    x_peers = [{"ctx": i, "kvh": yl * 4 + p} for p in x_places]

    barrier = pltpu.get_barrier_semaphore()
    for peer in [sibling] + y_peers + x_peers:
        pl.semaphore_signal(barrier, inc=1, device_id=peer, device_id_type=MESH)
    for t in range(1, 8):
        pl.semaphore_signal(
            barrier, inc=1, device_id={"ctx": ring(z + t) * 4 + r, "kvh": j}, device_id_type=MESH
        )

    kv[0, z, yh, c] = k_ref[...]
    kv[1, z, yh, c] = v_ref[...]
    for layer in range(2):
        w_all[layer, yl, z, c] = w_ref[layer, pl.ds(pl.multiple_of(yl * 80, 16), 80), :]
        for h in range(PAIRS):
            qs[layer * PAIRS + h] = q_ref[layer, :, h * 128 : (h + 1) * 128]
            dos[layer * PAIRS + h] = do_ref[layer, :, h * 128 : (h + 1) * 128]
    dkv[...] = jnp.zeros_like(dkv)
    pl.semaphore_wait(barrier, 14)

    def origin(way, n):
        step = n // 2 + 1
        return ring(z - step) if way == 0 else ring(z + step)

    reach = [2, 2, 1, 1, 3, 3, 4]

    def kv_arrival(way, n):
        return (way + n) % 2, ring(z - reach[n]) if way == 0 else ring(z + reach[n])

    def kv_hop(way, n):
        if n < 4:
            part, zz = (way + n) % 2, z
        else:
            part, zz = kv_arrival(way, n - 4 if n < 6 else 0)
        ref = kv.at[part, zz, yh, c]
        jump = 2 if n in (0, 1, 6) else 1
        target = {"ctx": (ring(z + jump) if way == 0 else ring(z - jump)) * 4 + r, "kvh": j}
        return send(ref, ref, kv_s.at[0], kv_r.at[way, n], target)

    def kv_wait(way, n):
        part, zz = kv_arrival(way, n)
        ref = kv.at[part, zz, yh, c]
        send(ref, ref, kv_s.at[0], kv_r.at[way, n], sides[way]).wait_recv()

    def kv_y(n, part, zz, place):
        ref = kv.at[part, zz, place, c]
        return send(ref, ref, ky_s.at[0], ky_r.at[n], y_peers[0])

    def kv_c(part, zz, place):
        ref = kv.at[part, zz, place, c]
        return send(ref, ref, kc_s.at[0], kc_r.at[0], sibling)

    def flip_key(zz, place, core):
        kt[zz, 2 * place + core] = kv[0, zz, place, core].astype(F32).T.astype(BF)

    def w_half(way, n):
        return lax.rem(yl + (1 if way == 1 and n == 6 else n % 2), 2)

    def w_send(layer, way, n):
        if n < 2:
            zz = z
        else:
            zz = ring(z - n // 2) if way == 0 else ring(z + n // 2)
        ref = w_all.at[layer, w_half(way, n), zz, c]
        return send(ref, ref, w_s.at[0], w_r.at[layer, way, n], sides[way])

    def w_sib(layer, half, zz):
        ref = w_all.at[layer, half, zz, c]
        return send(ref, ref, wc_s.at[0], wc_r.at[layer], sibling)

    def poll(layer, n):
        for way in range(2):
            zz = origin(way, n)
            half = w_half(way, n)
            ref = w_all.at[layer, half, zz, c]
            send(ref, ref, w_s.at[0], w_r.at[layer, way, n], sides[way]).wait_recv()
            if n <= 3 or (way == 0 and n == 4):
                w_send(layer, way, n + 2).start()
            if way == 1 and n == 5:
                w_send(layer, way, 6).start()
            w_sib(layer, half, zz).start()
        if layer == 0 and n in (5, 6):
            for way in range(2):
                w_send(1, way, n - 5).start()
            w_sib(1, w_half(0, n - 5), z).start()

    def w_swap(layer):
        return send(
            w_ref.at[layer, pl.ds(pl.multiple_of((1 - yl) * 80, 16), 80), :],
            w_all.at[layer, yl, z, c],
            ws_s.at[0],
            ws_r.at[layer],
            y_peers[1],
        )

    for n in range(4):
        for way in range(2):
            kv_hop(way, n).start()
    for n in range(2):
        kv_y(n, n, z, yh).start()
        kv_c(n, z, yh).start()
    w_swap(0).start()
    flip_key(z, yh, c)

    def pieces(n):
        if n < 0:
            return [(0, 0, z), (1, 1, z)]
        return [(2 + 2 * n + way,) + kv_arrival(way, n) for way in range(2)]

    def relay(n):
        for m, part, zz in pieces(n):
            kv_y(m, part, zz, 1 - yh).wait_recv()
            kv_c(part, zz, 1 - yh).start()
        for m, part, zz in pieces(n):
            if part == 0:
                if n >= 0:
                    flip_key(zz, yh, c)
                flip_key(zz, 1 - yh, c)

    def arrive(n):
        for way in range(2):
            kv_wait(way, n)
            if n == 0:
                kv_hop(way, 6).start()
            if n < 2:
                kv_hop(way, n + 4).start()
            part, zz = kv_arrival(way, n)
            kv_y(2 + 2 * n + way, part, zz, yh).start()
            kv_c(part, zz, yh).start()

    arrive(0)
    arrive(1)
    for way in range(2):
        w_send(0, way, 0).start()
    w_sib(0, w_half(0, 0), z).start()
    relay(-1)
    arrive(2)
    arrive(3)
    w_swap(0).wait_recv()
    for way in range(2):
        w_send(0, way, 1).start()
    w_sib(0, w_half(0, 1), z).start()
    relay(0)
    arrive(4)
    relay(1)
    arrive(5)
    arrive(6)
    relay(2)
    relay(3)
    poll(0, 0)
    relay(4)
    w_swap(1).start()
    relay(5)
    relay(6)
    poll(0, 1)
    others = kv.at[:, :, :, 1 - c]
    send(others, others, kc_s.at[0], kc_r.at[0], sibling).wait_recv()
    for zz in range(8):
        for spot in range(2):
            flip_key(zz, spot, 1 - c)
    poll(0, 2)
    w_swap(1).wait_recv()

    last = lax.div(z, 4)
    lane = lax.broadcasted_iota(jnp.int32, (SUB, 256), 1)
    place = z * 512 + r * 128 + lax.rem(lane, 128)

    def a_send(h, t):
        ref = a_all.at[pl.ds(2 * h, 2), yl, yh]
        return send(ref, ref, a_s.at[t], a_r.at[lax.div(h, 3), t], y_peers[t])

    def x_send(layer, t):
        return send(ct.at[layer, :, x_places[t]], xr.at[t, layer], x_s.at[0], x_r.at[layer], x_peers[t])

    def project(layer):
        part = pl.ds(0, 6) if layer == 0 else pl.ds(6, 4)
        for t, (ph, pw) in enumerate(y_places):
            ref = a_all.at[part, pw, ph]
            send(ref, ref, a_s.at[t], a_r.at[layer, t], y_peers[t]).wait_recv()
        ref = w_all.at[layer, :, :, 1 - c]
        send(ref, ref, wc_s.at[0], wc_r.at[layer], sibling).wait_recv()
        rows = [
            jnp.concatenate([a_all[layer * PAIRS + h, w].reshape(256, 128) for h in range(PAIRS)], axis=1)
            for w in range(2)
        ]
        for hi in range(2):
            total = dot_nt(w_all[layer, 0, 4 * hi : 4 * hi + 4].reshape(640, 640), rows[0])
            total = total + dot_nt(w_all[layer, 1, 4 * hi : 4 * hi + 4].reshape(640, 640), rows[1])
            ct[layer, hi] = total.astype(BF).reshape(4, 2, 80, 256)
        for t in range(3):
            x_send(layer, t).start()

    def pair(h, carry):
        two = pl.ds(2 * h, 2)
        query = qs[two].reshape(256, 128)
        cotangent = dos[two].reshape(256, 128)

        def forward(b, state, masked=False):
            m, total, weighted = state
            for n in range(PARTS):
                rows = pl.ds(n * SUB, SUB)
                zz = 4 * b + n // 4
                s = dot_nt(kv[0, zz, n // 2 % 2, n % 2], query)
                if masked:
                    key_place = lax.broadcasted_iota(jnp.int32, (SUB, 256), 0) + (b * BLOCK + n * SUB)
                    s = jnp.where(key_place <= place, s, LOWEST)
                d = dot_nt(kv[1, zz, n // 2 % 2, n % 2], cotangent)
                s = s.reshape(SUB // 8, 8, 256)
                peak = jnp.max(s, axis=0)
                e = jnp.exp2((s - peak[None]) * LOG2)
                part_total = jnp.sum(e, axis=0)
                part_weighted = jnp.sum(e * d.reshape(SUB // 8, 8, 256), axis=0)
                e_ref[b, rows] = e.reshape(SUB, 256)
                d_ref[b, rows] = d
                peaks[b, n] = peak
                new = jnp.maximum(m, peak)
                f0 = jnp.exp2((m - new) * LOG2)
                f1 = jnp.exp2((peak - new) * LOG2)
                total = total * f0 + part_total * f1
                weighted = weighted * f0 + part_weighted * f1
                m = new
            return m, total, weighted

        zero = jnp.zeros((8, 256), F32)
        state = lax.fori_loop(0, last, forward, (jnp.full((8, 256), LOWEST, F32), zero, zero))
        m8, total8, weighted8 = forward(last, state, True)
        for n, (layer, chunk) in enumerate(((0, 3), (0, 5), (1, 0), (1, 2), (1, 4))):
            pl.when(h == n)(lambda: poll(layer, chunk))
        m = jnp.max(m8, axis=0, keepdims=True)
        f = jnp.exp2((m8 - m) * LOG2)
        inverse = 1.0 / jnp.sum(total8 * f, axis=0, keepdims=True)
        delta = jnp.sum(weighted8 * f, axis=0, keepdims=True) * inverse

        def backward(b, dq):
            probs = []
            mixed = []
            for n in range(PARTS):
                rows = pl.ds(n * SUB, SUB)
                f = jnp.exp2((peaks[b, n] - m) * LOG2) * inverse
                p = (e_ref[b, rows].reshape(SUB // 8, 8, 256) * f[None]).reshape(SUB, 256)
                mixed.append((p * (d_ref[b, rows] - delta)).astype(BF))
                probs.append(p.astype(BF))
            probs = jnp.concatenate(probs, 0)
            mixed = jnp.concatenate(mixed, 0)
            here = pl.ds(4 * b, 4)
            shape = (4, 2, 2, 128, 128)
            dkv[1, here] += dot(probs, cotangent).reshape(shape)
            dkv[0, here] += dot(mixed, query).reshape(shape)
            keys = jnp.concatenate([kt[4 * b + n // 4, n % 4] for n in range(PARTS)], axis=1)
            return dq + dot(keys, mixed)

        dq = lax.fori_loop(0, last + 1, backward, jnp.zeros((128, 256), F32))
        for u in range(2):
            a_all[2 * h + u, yl, yh] = (dq[:, u * 128 : (u + 1) * 128].T * SCALE).astype(BF)
        for t in range(3):
            a_send(h, t).start()
        for n, (layer, chunk) in enumerate(((0, 4), (0, 6), (1, 1), (1, 3))):
            pl.when(h == n)(lambda: poll(layer, chunk))
        pl.when(h == 3)(lambda: project(0))
        return carry

    lax.fori_loop(0, PAIRS, pair, 0)

    def s_send(zz):
        return send(sb.at[:, zz], sbr.at[:, zz], s_s.at[zz], s_r.at[zz], sibling)

    def y_send(zz):
        return send(yb.at[:, zz], ybr.at[:, zz], y_s.at[zz], y_r.at[zz], y_peers[0])

    def stage_sibling(zz, carry):
        sb[0, zz] = (dkv[0, zz, :, 1 - c] * SCALE).astype(BF)
        sb[1, zz] = dkv[1, zz, :, 1 - c].astype(BF)
        s_send(zz).start()
        return carry

    lax.fori_loop(0, z + 1, stage_sibling, 0)

    def stage_y(zz, carry):
        s_send(zz).wait_recv()
        for n, scale in ((0, SCALE), (1, 1.0)):
            far = dkv[n, zz, 1 - yh, c] * scale + sbr[n, zz, 1 - yh].astype(F32)
            yb[n, zz] = far.astype(BF)
        y_send(zz).start()
        for n, scale in ((0, SCALE), (1, 1.0)):
            dkv[n, zz, yh, c] = dkv[n, zz, yh, c] * scale + sbr[n, zz, yh].astype(F32)
        return carry

    lax.fori_loop(0, z + 1, stage_y, 0)

    def finish(layer):
        ref = xr.at[:, layer]
        send(ref, ref, x_s.at[0], x_r.at[layer], sibling).wait_recv()
        total = ct[layer, :, x].astype(F32)
        for t in range(3):
            total = total + xr[t, layer].astype(F32)
        total = total.astype(BF)
        for half in range(2):
            fs[half, :, layer] = total[..., half * 128 : (half + 1) * 128]
        for t in range(3):
            f_send(layer, t).start()
        fr[layer, yh, :, yl] = fs[yh, yl, layer]

    def f_send(layer, t):
        ph, pw = y_places[t]
        return send(
            fs.at[ph, pw, layer], fr.at[layer, yh, :, yl], f_s.at[layer, t], f_r.at[layer, t], y_peers[t]
        )

    poll(1, 5)
    finish(0)
    poll(1, 6)
    project(1)

    def stage_z(zz, carry):
        y_send(zz).wait_recv()
        for n in range(2):
            near = dkv[n, zz, yh, c] + ybr[n, zz].astype(F32)
            dkv[n, zz, yh, c] = near
            zb[n, zz] = near.astype(BF)

        @pl.when(zz < z)
        def _():
            send(
                zb.at[:, zz], zr.at[:, z], z_s.at[zz], z_r.at[z], {"ctx": zz * 4 + r, "kvh": j}
            ).start()

        return carry

    early = jnp.minimum(z + 1, 5)
    lax.fori_loop(0, early, stage_z, 0)
    finish(1)
    lax.fori_loop(early, z + 1, stage_z, 0)

    def result(layer):
        for t in range(3):
            f_send(layer, t).wait_recv()
        out_ref[layer] = fr[layer].reshape(640, 128).astype(F32).T.astype(BF)

    result(0)

    def gather_z(zz, carry):
        send(zb.at[:, z], zr.at[:, zz], z_s.at[z], z_r.at[zz], sides[0]).wait_recv()
        for n in range(2):
            dkv[n, z, yh, c] += zr[n, zz].astype(F32)
        return carry

    lax.fori_loop(z + 1, 8, gather_z, 0)
    gk_ref[...] = dkv[0, z, yh, c].astype(BF)
    gv_ref[...] = dkv[1, z, yh, c].astype(BF)
    result(1)

    for sem, ref in (
        (kv_s.at[0], kv.at[0, pl.ds(0, 7), :, 0]),
        (ky_s.at[0], kv.at[0, :, :, 0]),
        (kc_s.at[0], kv.at[0]),
        (w_s.at[0], w_all.at[:, :, pl.ds(0, 7), 0]),
        (wc_s.at[0], w_all.at[:, :, :, 0]),
        (ws_s.at[0], w_all.at[:, 0, 0, 0]),
        (x_s.at[0], xr),
        (a_s.at[0], a_all.at[:, 0, 0]),
        (a_s.at[1], a_all.at[:, 0, 0]),
        (a_s.at[2], a_all.at[:, 0, 0]),
    ):
        send(ref, ref, sem, kc_r.at[0], sibling).wait_send()
    for layer in range(2):
        for t in range(3):
            f_send(layer, t).wait_send()

    def drain(zz, carry):
        s_send(zz).wait_send()
        y_send(zz).wait_send()

        @pl.when(zz < z)
        def _():
            send(zb.at[:, zz], zr.at[:, z], z_s.at[zz], z_r.at[z], sides[0]).wait_send()

        return carry

    lax.fori_loop(0, z + 1, drain, 0)


def body(queries, keys, values, grad_out, query_weight):
    dma = pltpu.SemaphoreType.DMA
    vmem = pltpu.VMEM
    return pl.pallas_call(
        kernel,
        out_shape=(
            jax.ShapeDtypeStruct((2, 128, 640), BF),
            jax.ShapeDtypeStruct((128, 128), BF),
            jax.ShapeDtypeStruct((128, 128), BF),
        ),
        in_specs=[pl.BlockSpec(memory_space=pltpu.VMEM)] * 5,
        out_specs=[pl.BlockSpec(memory_space=pltpu.VMEM)] * 3,
        scratch_shapes=[
            vmem((2, 8, 2, 2, 128, 128), BF),
            vmem((8, 4, 128, 128), BF),
            vmem((2, BLOCK, 256), F32),
            vmem((2, BLOCK, 256), F32),
            vmem((2, PARTS, 8, 256), F32),
            vmem((10, 128, 128), BF),
            vmem((10, 128, 128), BF),
            vmem((2, 8, 2, 2, 128, 128), F32),
            vmem((2, 2, 8, 2, 80, 640), BF),
            vmem((10, 2, 2, 128, 128), BF),
            vmem((2, 2, 4, 2, 80, 256), BF),
            vmem((3, 2, 2, 2, 80, 256), BF),
            vmem((2, 2, 2, 2, 80, 128), BF),
            vmem((2, 2, 2, 2, 80, 128), BF),
            vmem((2, 8, 2, 128, 128), BF),
            vmem((2, 8, 2, 128, 128), BF),
            vmem((2, 8, 128, 128), BF),
            vmem((2, 8, 128, 128), BF),
            vmem((2, 8, 128, 128), BF),
            vmem((2, 8, 128, 128), BF),
            dma((1,)), dma((2, 7)), dma((1,)), dma((16,)), dma((1,)), dma((1,)),
            dma((1,)), dma((2,)), dma((1,)), dma((2, 2, 7)), dma((1,)), dma((2,)),
            dma((3,)), dma((2, 3)), dma((1,)), dma((2,)), dma((2, 3)), dma((2, 3)),
            dma((8,)), dma((8,)), dma((8,)), dma((8,)), dma((8,)), dma((8,)),
        ],
        compiler_params=pltpu.CompilerParams(
            collective_id=0, has_side_effects=True, vmem_limit_bytes=56 << 20
        ),
    )(queries, keys, values, grad_out, query_weight)


def solution(mesh):
    cols = P(None, "ctx", "kvh")
    flat = P("ctx", "kvh")
    return jax.shard_map(
        body,
        mesh=mesh,
        in_specs=(cols, flat, flat, cols, cols),
        out_specs=(cols, flat, flat),
        check_vma=False,
    )
```

time: 98.4 us -> 82.3 us (0.84)
  Pallas kernels: 94.5 us -> 78 us
    pallas_call x1, Pallas kernels: 94.5 us -> 78 us  [body(): pl.pallas_call(kernel, out_shape=(jax.ShapeDtypeStruct((2, 128, 640), BF)...]
where the time goes in v2:
time: 82.3 us; the launch traced here: 81.8 us
  Pallas kernels  78 us (95%)
  local copies, waits for them, and re-layouts  3.12 us (4%)
    pallas_call x1, Pallas kernels, body(): pl.pallas_call(kernel, out_shape=(jax.ShapeDtypeStruct((2, 128, 640), BF)...  78 us
    unnamed x7, local copies, waits for them, and re-layouts  3.12 us

profile of v2, /device:TPU:1, one launch (start us, length us, event | category | flops | bytes accessed | tf_op | source)
XLA Modules:
  0.0 81.8 jit_solution(13534086952301409965)
XLA Ops:
  0.6 78.0 %shard_map.76 = (bf16[2,128,640]{2,1,0:T(8,128)(2,1)}, bf16[128,128]{1,0:T(8,128)(2,1)}, bf16[128,128]{1,0:T(8,128)(2,1)}) custom-call(bf16[2,128,640]{2,1,0:T(8,128)(2,1)} %q_ref.1, bf16[128,128]{1,0:T(8,128)(2,1)} %k_ref.1, bf16[128,128]{1,0:T(8,128)(2,1)} %v_ref.1, bf16[2,128,640]{2,1,0:T(8,128)(2,1)} %do_ref.1, bf16[2,160,640]{2,1,0:T(8,128)(2,1)} %w_ref.1), custom_call_target="tpu_custom_call" | custom-call | tf_op jit(solution)/shard_map/pallas_call | solution.py:453
  78.6 0.0 copy-start.1
  78.6 1.7 %copy.11 = bf16[2,128,640]{2,1,0:T(8,128)(2,1)} copy(bf16[2,128,640]{2,1,0:T(8,128)(2,1)} %get-tuple-element.6) | data formatting | bytes 655360
  80.4 0.0 copy-done.1
  80.4 0.0 copy-start
  80.4 0.6 copy.12
  81.0 0.2 copy-done
  81.1 0.6 copy.13
Async XLA Ops:
  78.6 1.7 %copy-start.1 = (bf16[128,128]{1,0:T(8,128)(2,1)S(1)}, bf16[128,128]{1,0:T(8,128)(2,1)}, u32[]{:S(2)}) copy-start(bf16[128,128]{1,0:T(8,128)(2,1)} %get-tuple-element.7) | copy-start | bytes 98308
  80.4 0.8 copy-start

commit v3 on v2

--- a/solution.py
+++ b/solution.py
@@ -39,7 +39,7 @@
 
 def kernel(
     q_ref, k_ref, v_ref, do_ref, w_ref,
-    out_ref, gk_ref, gv_ref,
+    turned_ref, both_ref,
     kv, kt, e_ref, d_ref, peaks, qs, dos, dkv, w_all, a_all, ct, xr, fs, fr,
     sb, sbr, yb, ybr, zb, zr,
     kv_s, kv_r, ky_s, ky_r, kc_s, kc_r,
@@ -86,9 +86,8 @@
     dkv[...] = jnp.zeros_like(dkv)
     pl.semaphore_wait(barrier, 14)
 
-    def origin(way, n):
-        step = n // 2 + 1
-        return ring(z - step) if way == 0 else ring(z + step)
+    def shift(way, d):
+        return ring(z - d) if way == 0 else ring(z + d)
 
     reach = [2, 2, 1, 1, 3, 3, 4]
 
@@ -121,36 +120,36 @@
     def flip_key(zz, place, core):
         kt[zz, 2 * place + core] = kv[0, zz, place, core].astype(F32).T.astype(BF)
 
-    def w_half(way, n):
-        return lax.rem(yl + (1 if way == 1 and n == 6 else n % 2), 2)
+    def w_half(layer, way, n):
+        if layer == 0:
+            return lax.rem(yl + (1 if way == 1 and n == 6 else n % 2), 2)
+        return lax.rem(yl + way + n, 2)
+
+    def w_ref_of(layer, way, n, zz):
+        return w_all.at[layer, w_half(layer, way, n), zz, c]
 
     def w_send(layer, way, n):
-        if n < 2:
-            zz = z
-        else:
-            zz = ring(z - n // 2) if way == 0 else ring(z + n // 2)
-        ref = w_all.at[layer, w_half(way, n), zz, c]
+        ref = w_ref_of(layer, way, n, z if n < 2 else shift(way, n // 2))
         return send(ref, ref, w_s.at[0], w_r.at[layer, way, n], sides[way])
 
-    def w_sib(layer, half, zz):
-        ref = w_all.at[layer, half, zz, c]
-        return send(ref, ref, wc_s.at[0], wc_r.at[layer], sibling)
+    def w_sib(ref, group):
+        return send(ref, ref, wc_s.at[0], wc_r.at[group], sibling)
+
+    def own_weight(layer, n):
+        for way in range(2):
+            w_send(layer, way, n).start()
+        w_sib(w_ref_of(layer, 0, n, z), layer).start()
 
     def poll(layer, n):
         for way in range(2):
-            zz = origin(way, n)
-            half = w_half(way, n)
-            ref = w_all.at[layer, half, zz, c]
+            ref = w_ref_of(layer, way, n, shift(way, n // 2 + 1))
             send(ref, ref, w_s.at[0], w_r.at[layer, way, n], sides[way]).wait_recv()
-            if n <= 3 or (way == 0 and n == 4):
-                w_send(layer, way, n + 2).start()
-            if way == 1 and n == 5:
-                w_send(layer, way, 6).start()
-            w_sib(layer, half, zz).start()
-        if layer == 0 and n in (5, 6):
-            for way in range(2):
-                w_send(1, way, n - 5).start()
-            w_sib(1, w_half(0, n - 5), z).start()
+            last_from = 5 if layer == 0 and way == 1 else 4
+            if n < 4 or n == last_from:
+                w_send(layer, way, 6 if n == last_from else n + 2).start()
+            w_sib(ref, 2 if layer == 1 and n > 3 else layer).start()
+        if layer == 0 and n in (3, 4):
+            own_weight(1, n - 3)
 
     def w_swap(layer):
         return send(
@@ -168,6 +167,7 @@
         kv_y(n, n, z, yh).start()
         kv_c(n, z, yh).start()
     w_swap(0).start()
+    own_weight(0, 0)
     flip_key(z, yh, c)
 
     def pieces(n):
@@ -198,36 +198,33 @@
 
     arrive(0)
     arrive(1)
-    for way in range(2):
-        w_send(0, way, 0).start()
-    w_sib(0, w_half(0, 0), z).start()
     relay(-1)
     arrive(2)
     arrive(3)
     w_swap(0).wait_recv()
-    for way in range(2):
-        w_send(0, way, 1).start()
-    w_sib(0, w_half(0, 1), z).start()
+    own_weight(0, 1)
     relay(0)
+    poll(0, 0)
+    relay(1)
     arrive(4)
-    relay(1)
     arrive(5)
     arrive(6)
     relay(2)
+    poll(0, 1)
+    w_swap(1).start()
     relay(3)
-    poll(0, 0)
+    poll(0, 2)
     relay(4)
-    w_swap(1).start()
+    w_swap(1).wait_recv()
+    poll(0, 3)
     relay(5)
     relay(6)
-    poll(0, 1)
+    poll(0, 4)
     others = kv.at[:, :, :, 1 - c]
     send(others, others, kc_s.at[0], kc_r.at[0], sibling).wait_recv()
     for zz in range(8):
         for spot in range(2):
             flip_key(zz, spot, 1 - c)
-    poll(0, 2)
-    w_swap(1).wait_recv()
 
     last = lax.div(z, 4)
     lane = lax.broadcasted_iota(jnp.int32, (SUB, 256), 1)
@@ -240,23 +237,48 @@
     def x_send(layer, t):
         return send(ct.at[layer, :, x_places[t]], xr.at[t, layer], x_s.at[0], x_r.at[layer], x_peers[t])
 
-    def project(layer):
+    def wait_rows(layer):
         part = pl.ds(0, 6) if layer == 0 else pl.ds(6, 4)
         for t, (ph, pw) in enumerate(y_places):
             ref = a_all.at[part, pw, ph]
             send(ref, ref, a_s.at[t], a_r.at[layer, t], y_peers[t]).wait_recv()
-        ref = w_all.at[layer, :, :, 1 - c]
-        send(ref, ref, wc_s.at[0], wc_r.at[layer], sibling).wait_recv()
-        rows = [
-            jnp.concatenate([a_all[layer * PAIRS + h, w].reshape(256, 128) for h in range(PAIRS)], axis=1)
-            for w in range(2)
-        ]
+
+    def wait_weights(group, ref):
+        send(ref, ref, wc_s.at[0], wc_r.at[group], sibling).wait_recv()
+
+    def gathered(layer, w):
+        return jnp.concatenate([a_all[layer * PAIRS + h, w].reshape(256, 128) for h in range(PAIRS)], axis=1)
+
+    def first_layer():
+        wait_rows(0)
+        wait_weights(0, w_all.at[0, :, :, 1 - c])
+        rows = [gathered(0, w) for w in range(2)]
         for hi in range(2):
-            total = dot_nt(w_all[layer, 0, 4 * hi : 4 * hi + 4].reshape(640, 640), rows[0])
-            total = total + dot_nt(w_all[layer, 1, 4 * hi : 4 * hi + 4].reshape(640, 640), rows[1])
-            ct[layer, hi] = total.astype(BF).reshape(4, 2, 80, 256)
+            total = dot_nt(w_all[0, 0, 4 * hi : 4 * hi + 4].reshape(640, 640), rows[0])
+            total = total + dot_nt(w_all[0, 1, 4 * hi : 4 * hi + 4].reshape(640, 640), rows[1])
+            ct[0, hi] = total.astype(BF).reshape(4, 2, 80, 256)
         for t in range(3):
-            x_send(layer, t).start()
+            x_send(0, t).start()
+
+    def second_layer(planes):
+        rows = [gathered(1, w) for w in range(2)]
+        for zz in planes:
+            total = dot_nt(w_all[1, 0, zz].reshape(160, 640), rows[0])
+            total = total + dot_nt(w_all[1, 1, zz].reshape(160, 640), rows[1])
+            hi = lax.div(zz, 4)
+            p = lax.rem(zz, 4)
+            ct[1, hi, p] = total.astype(BF).reshape(2, 80, 256)
+            t = lax.rem(p - x + 4, 4)
+
+            @pl.when(t > 0)
+            def _():
+                send(
+                    ct.at[1, hi, p],
+                    xr.at[t - 1, 1, hi],
+                    x_s.at[0],
+                    x_r.at[1],
+                    {"ctx": i, "kvh": yl * 4 + p},
+                ).start()
 
     def pair(h, carry):
         two = pl.ds(2 * h, 2)
@@ -292,7 +314,7 @@
         zero = jnp.zeros((8, 256), F32)
         state = lax.fori_loop(0, last, forward, (jnp.full((8, 256), LOWEST, F32), zero, zero))
         m8, total8, weighted8 = forward(last, state, True)
-        for n, (layer, chunk) in enumerate(((0, 3), (0, 5), (1, 0), (1, 2), (1, 4))):
+        for n, (layer, chunk) in ((1, (0, 6)), (3, (1, 2)), (4, (1, 3))):
             pl.when(h == n)(lambda: poll(layer, chunk))
         m = jnp.max(m8, axis=0, keepdims=True)
         f = jnp.exp2((m8 - m) * LOG2)
@@ -322,9 +344,9 @@
             a_all[2 * h + u, yl, yh] = (dq[:, u * 128 : (u + 1) * 128].T * SCALE).astype(BF)
         for t in range(3):
             a_send(h, t).start()
-        for n, (layer, chunk) in enumerate(((0, 4), (0, 6), (1, 1), (1, 3))):
+        for n, (layer, chunk) in enumerate(((0, 5), (1, 0), (1, 1))):
             pl.when(h == n)(lambda: poll(layer, chunk))
-        pl.when(h == 3)(lambda: project(0))
+        pl.when(h == 3)(first_layer)
         return carry
 
     lax.fori_loop(0, PAIRS, pair, 0)
@@ -341,7 +363,6 @@
         s_send(zz).start()
         return carry
 
-    lax.fori_loop(0, z + 1, stage_sibling, 0)
 
     def stage_y(zz, carry):
         s_send(zz).wait_recv()
@@ -353,7 +374,29 @@
             dkv[n, zz, yh, c] = dkv[n, zz, yh, c] * scale + sbr[n, zz, yh].astype(F32)
         return carry
 
-    lax.fori_loop(0, z + 1, stage_y, 0)
+    def stage_z(zz, carry):
+        y_send(zz).wait_recv()
+        for n in range(2):
+            near = dkv[n, zz, yh, c] + ybr[n, zz].astype(F32)
+            dkv[n, zz, yh, c] = near
+            zb[n, zz] = near.astype(BF)
+
+        @pl.when(zz < z)
+        def _():
+            send(
+                zb.at[:, zz], zr.at[:, z], z_s.at[zz], z_r.at[z], {"ctx": zz * 4 + r, "kvh": j}
+            ).start()
+
+        return carry
+
+    def stage_both(zz, carry):
+        stage_sibling(zz, carry)
+        pl.when(zz > 1)(lambda: stage_y(zz - 2, None))
+        return carry
+
+    lax.fori_loop(0, z + 1, stage_both, 0)
+    poll(1, 4)
+    lax.fori_loop(jnp.maximum(z - 1, 0), z + 1, stage_y, 0)
 
     def finish(layer):
         ref = xr.at[:, layer]
@@ -374,35 +417,26 @@
             fs.at[ph, pw, layer], fr.at[layer, yh, :, yl], f_s.at[layer, t], f_r.at[layer, t], y_peers[t]
         )
 
+    wait_rows(1)
+    wait_weights(1, w_all.at[0, :, pl.ds(0, 5), 0])
+    second_layer([z, shift(0, 1), shift(1, 1), shift(0, 2), shift(1, 2)])
+    early = jnp.minimum(z + 1, 2)
+    lax.fori_loop(0, early, stage_z, 0)
     poll(1, 5)
+    poll(1, 6)
+    wait_weights(2, w_all.at[0, :, pl.ds(0, 3), 0])
+    second_layer([shift(0, 3), shift(1, 3), shift(0, 4)])
     finish(0)
-    poll(1, 6)
-    project(1)
-
-    def stage_z(zz, carry):
-        y_send(zz).wait_recv()
-        for n in range(2):
-            near = dkv[n, zz, yh, c] + ybr[n, zz].astype(F32)
-            dkv[n, zz, yh, c] = near
-            zb[n, zz] = near.astype(BF)
-
-        @pl.when(zz < z)
-        def _():
-            send(
-                zb.at[:, zz], zr.at[:, z], z_s.at[zz], z_r.at[z], {"ctx": zz * 4 + r, "kvh": j}
-            ).start()
-
-        return carry
-
-    early = jnp.minimum(z + 1, 5)
-    lax.fori_loop(0, early, stage_z, 0)
+
+    middle = jnp.minimum(z + 1, 6)
+    lax.fori_loop(early, middle, stage_z, 0)
     finish(1)
-    lax.fori_loop(early, z + 1, stage_z, 0)
+    lax.fori_loop(middle, z + 1, stage_z, 0)
 
     def result(layer):
         for t in range(3):
             f_send(layer, t).wait_recv()
-        out_ref[layer] = fr[layer].reshape(640, 128).astype(F32).T.astype(BF)
+        turned_ref[layer] = fr[layer].reshape(640, 128)
 
     result(0)
 
@@ -413,8 +447,8 @@
         return carry
 
     lax.fori_loop(z + 1, 8, gather_z, 0)
-    gk_ref[...] = dkv[0, z, yh, c].astype(BF)
-    gv_ref[...] = dkv[1, z, yh, c].astype(BF)
+    for n in range(2):
+        both_ref[n] = dkv[n, z, yh, c].astype(BF)
     result(1)
 
     for sem, ref in (
@@ -447,18 +481,21 @@
     lax.fori_loop(0, z + 1, drain, 0)
 
 
+def outputs_kernel(turned_ref, both_ref, out_ref, gk_ref, gv_ref):
+    for layer in range(2):
+        out_ref[layer] = turned_ref[layer].astype(F32).T.astype(BF)
+    gk_ref[...] = both_ref[0]
+    gv_ref[...] = both_ref[1]
+
+
 def body(queries, keys, values, grad_out, query_weight):
     dma = pltpu.SemaphoreType.DMA
     vmem = pltpu.VMEM
-    return pl.pallas_call(
+    turned, both = pl.pallas_call(
         kernel,
-        out_shape=(
-            jax.ShapeDtypeStruct((2, 128, 640), BF),
-            jax.ShapeDtypeStruct((128, 128), BF),
-            jax.ShapeDtypeStruct((128, 128), BF),
-        ),
+        out_shape=(jax.ShapeDtypeStruct((2, 640, 128), BF), jax.ShapeDtypeStruct((2, 128, 128), BF)),
         in_specs=[pl.BlockSpec(memory_space=pltpu.VMEM)] * 5,
-        out_specs=[pl.BlockSpec(memory_space=pltpu.VMEM)] * 3,
+        out_specs=[pl.BlockSpec(memory_space=pltpu.VMEM)] * 2,
         scratch_shapes=[
             vmem((2, 8, 2, 2, 128, 128), BF),
             vmem((8, 4, 128, 128), BF),
@@ -481,7 +518,7 @@
             vmem((2, 8, 128, 128), BF),
             vmem((2, 8, 128, 128), BF),
             dma((1,)), dma((2, 7)), dma((1,)), dma((16,)), dma((1,)), dma((1,)),
-            dma((1,)), dma((2,)), dma((1,)), dma((2, 2, 7)), dma((1,)), dma((2,)),
+            dma((1,)), dma((2,)), dma((1,)), dma((2, 2, 7)), dma((1,)), dma((3,)),
             dma((3,)), dma((2, 3)), dma((1,)), dma((2,)), dma((2, 3)), dma((2, 3)),
             dma((8,)), dma((8,)), dma((8,)), dma((8,)), dma((8,)), dma((8,)),
         ],
@@ -489,6 +526,16 @@
             collective_id=0, has_side_effects=True, vmem_limit_bytes=56 << 20
         ),
     )(queries, keys, values, grad_out, query_weight)
+    return pl.pallas_call(
+        outputs_kernel,
+        out_shape=(
+            jax.ShapeDtypeStruct((2, 128, 640), BF),
+            jax.ShapeDtypeStruct((128, 128), BF),
+            jax.ShapeDtypeStruct((128, 128), BF),
+        ),
+        in_specs=[pl.BlockSpec(memory_space=pltpu.VMEM)] * 2,
+        out_specs=[pl.BlockSpec(memory_space=pltpu.VMEM)] * 3,
+    )(turned, both)
 
 
 def solution(mesh):

time: 82.3 us -> 79.5 us (0.966)
  local copies, waits for them, and re-layouts: 3.12 us -> 0 us
    unnamed x7 -> x0, local copies, waits for them, and re-layouts: 3.12 us -> none
    pallas_call x1 -> x2, Pallas kernels: 78 us -> 78.7 us  [the longest x1 76.8 us: body(): pl.pallas_call(kernel, out_shape=(jax.ShapeDtypeStruct((2, 640, 128), BF)...]
where the time goes in v3:
time: 79.5 us; the launch traced here: 79.3 us
  Pallas kernels  78.7 us (99%)
    pallas_call x1, Pallas kernels, body(): pl.pallas_call(kernel, out_shape=(jax.ShapeDtypeStruct((2, 640, 128), BF)...  76.8 us
    pallas_call x1, Pallas kernels, body(): pl.pallas_call(outputs_kernel, out_shape=(jax.ShapeDtypeStruct((2, 128, 6...  1.88 us

profile of v3, /device:TPU:1, one launch (start us, length us, event | category | flops | bytes accessed | tf_op | source)
XLA Modules:
  0.0 79.3 jit_solution(786325337901941325)
XLA Ops:
  0.6 76.8 %shard_map.76 = (bf16[2,640,128]{2,1,0:T(8,128)(2,1)}, bf16[2,128,128]{2,1,0:T(8,128)(2,1)}) custom-call(bf16[2,128,640]{2,1,0:T(8,128)(2,1)} %q_ref.1, bf16[128,128]{1,0:T(8,128)(2,1)} %k_ref.1, bf16[128,128]{1,0:T(8,128)(2,1)} %v_ref.1, bf16[2,128,640]{2,1,0:T(8,128)(2,1)} %do_ref.1, bf16[2,160,640]{2,1,0:T(8,128)(2,1)} %w_ref.1), custom_call_target="tpu_custom_call" | custom-call | tf_op jit(solution)/shard_map/pallas_call | solution.py:494
  77.5 1.9 %shard_map.77 = (bf16[2,128,640]{2,1,0:T(8,128)(2,1)}, bf16[128,128]{1,0:T(8,128)(2,1)}, bf16[128,128]{1,0:T(8,128)(2,1)}) custom-call(bf16[2,640,128]{2,1,0:T(8,128)(2,1)} %get-tuple-element.5.turned_ref, bf16[2,128,128]{2,1,0:T(8,128)(2,1)} %get-tuple-element.6.both_ref), custom_call_target="tpu_custom_call" | custom-call | tf_op jit(solution)/shard_map/pallas_call | solution.py:529

commit v4 on v3

--- a/solution.py
+++ b/solution.py
@@ -45,7 +45,7 @@
     kv_s, kv_r, ky_s, ky_r, kc_s, kc_r,
     ws_s, ws_r, w_s, w_r, wc_s, wc_r,
     a_s, a_r, x_s, x_r, f_s, f_r,
-    s_s, s_r, y_s, y_r, z_s, z_r,
+    s_s, s_r, y_s, y_r, z_s, z_r, in_s,
 ):
     i = lax.axis_index("ctx")
     j = lax.axis_index("kvh")
@@ -76,14 +76,24 @@
             barrier, inc=1, device_id={"ctx": ring(z + t) * 4 + r, "kvh": j}, device_id_type=MESH
         )
 
-    kv[0, z, yh, c] = k_ref[...]
-    kv[1, z, yh, c] = v_ref[...]
+    loads = [
+        pltpu.make_async_copy(k_ref, kv.at[0, z, yh, c], in_s.at[0]),
+        pltpu.make_async_copy(v_ref, kv.at[1, z, yh, c], in_s.at[1]),
+        pltpu.make_async_copy(
+            w_ref.at[:, pl.ds(pl.multiple_of(yl * 80, 16), 80), :], w_all.at[:, yl, z, c], in_s.at[2]
+        ),
+    ]
+    for load in loads:
+        load.start()
     for layer in range(2):
-        w_all[layer, yl, z, c] = w_ref[layer, pl.ds(pl.multiple_of(yl * 80, 16), 80), :]
         for h in range(PAIRS):
-            qs[layer * PAIRS + h] = q_ref[layer, :, h * 128 : (h + 1) * 128]
-            dos[layer * PAIRS + h] = do_ref[layer, :, h * 128 : (h + 1) * 128]
+            column = pl.ds(h * 128, 128)
+            g = layer * PAIRS + h
+            pltpu.make_async_copy(q_ref.at[layer, :, column], qs.at[g], in_s.at[3]).start()
+            pltpu.make_async_copy(do_ref.at[layer, :, column], dos.at[g], in_s.at[4]).start()
     dkv[...] = jnp.zeros_like(dkv)
+    for load in loads:
+        load.wait()
     pl.semaphore_wait(barrier, 14)
 
     def shift(way, d):
@@ -226,6 +236,8 @@
         for spot in range(2):
             flip_key(zz, spot, 1 - c)
 
+    pltpu.make_async_copy(qs, qs, in_s.at[3]).wait()
+    pltpu.make_async_copy(dos, dos, in_s.at[4]).wait()
     last = lax.div(z, 4)
     lane = lax.broadcasted_iota(jnp.int32, (SUB, 256), 1)
     place = z * 512 + r * 128 + lax.rem(lane, 128)
@@ -314,7 +326,7 @@
         zero = jnp.zeros((8, 256), F32)
         state = lax.fori_loop(0, last, forward, (jnp.full((8, 256), LOWEST, F32), zero, zero))
         m8, total8, weighted8 = forward(last, state, True)
-        for n, (layer, chunk) in ((1, (0, 6)), (3, (1, 2)), (4, (1, 3))):
+        for n, (layer, chunk) in enumerate(((0, 5), (0, 6), (1, 0), (1, 1), (1, 3))):
             pl.when(h == n)(lambda: poll(layer, chunk))
         m = jnp.max(m8, axis=0, keepdims=True)
         f = jnp.exp2((m8 - m) * LOG2)
@@ -344,7 +356,7 @@
             a_all[2 * h + u, yl, yh] = (dq[:, u * 128 : (u + 1) * 128].T * SCALE).astype(BF)
         for t in range(3):
             a_send(h, t).start()
-        for n, (layer, chunk) in enumerate(((0, 5), (1, 0), (1, 1))):
+        for n, (layer, chunk) in ((3, (1, 2)),):
             pl.when(h == n)(lambda: poll(layer, chunk))
         pl.when(h == 3)(first_layer)
         return carry
@@ -494,7 +506,7 @@
     turned, both = pl.pallas_call(
         kernel,
         out_shape=(jax.ShapeDtypeStruct((2, 640, 128), BF), jax.ShapeDtypeStruct((2, 128, 128), BF)),
-        in_specs=[pl.BlockSpec(memory_space=pltpu.VMEM)] * 5,
+        in_specs=[pl.BlockSpec(memory_space=pl.ANY)] * 5,
         out_specs=[pl.BlockSpec(memory_space=pltpu.VMEM)] * 2,
         scratch_shapes=[
             vmem((2, 8, 2, 2, 128, 128), BF),
@@ -520,7 +532,7 @@
             dma((1,)), dma((2, 7)), dma((1,)), dma((16,)), dma((1,)), dma((1,)),
             dma((1,)), dma((2,)), dma((1,)), dma((2, 2, 7)), dma((1,)), dma((3,)),
             dma((3,)), dma((2, 3)), dma((1,)), dma((2,)), dma((2, 3)), dma((2, 3)),
-            dma((8,)), dma((8,)), dma((8,)), dma((8,)), dma((8,)), dma((8,)),
+            dma((8,)), dma((8,)), dma((8,)), dma((8,)), dma((8,)), dma((8,)), dma((5,)),
         ],
         compiler_params=pltpu.CompilerParams(
             collective_id=0, has_side_effects=True, vmem_limit_bytes=56 << 20

time: 79.5 us -> 78.1 us (0.982)
  Pallas kernels: 78.7 us -> 77.4 us
    pallas_call x1, Pallas kernels: 76.8 us -> 75.5 us  [body(): pl.pallas_call(kernel, out_shape=(jax.ShapeDtypeStruct((2, 640, 128), BF)...]
where the time goes in v4:
time: 78.1 us; the launch traced here: 78 us
  Pallas kernels  77.4 us (99%)
    pallas_call x1, Pallas kernels, body(): pl.pallas_call(kernel, out_shape=(jax.ShapeDtypeStruct((2, 640, 128), BF)...  75.5 us
    pallas_call x1, Pallas kernels, body(): pl.pallas_call(outputs_kernel, out_shape=(jax.ShapeDtypeStruct((2, 128, 6...  1.88 us

profile of v4, /device:TPU:1, one launch (start us, length us, event | category | flops | bytes accessed | tf_op | source)
XLA Modules:
  0.0 78.0 jit_solution(8920088945154032978)
XLA Ops:
  0.6 75.5 %shard_map.76 = (bf16[2,640,128]{2,1,0:T(8,128)(2,1)}, bf16[2,128,128]{2,1,0:T(8,128)(2,1)}) custom-call(bf16[2,128,640]{2,1,0:T(8,128)(2,1)} %q_ref.1, bf16[128,128]{1,0:T(8,128)(2,1)} %k_ref.1, bf16[128,128]{1,0:T(8,128)(2,1)} %v_ref.1, bf16[2,128,640]{2,1,0:T(8,128)(2,1)} %do_ref.1, bf16[2,160,640]{2,1,0:T(8,128)(2,1)} %w_ref.1), custom_call_target="tpu_custom_call" | custom-call | tf_op jit(solution)/shard_map/pallas_call | solution.py:506
  76.1 1.9 %shard_map.77 = (bf16[2,128,640]{2,1,0:T(8,128)(2,1)}, bf16[128,128]{1,0:T(8,128)(2,1)}, bf16[128,128]{1,0:T(8,128)(2,1)}) custom-call(bf16[2,640,128]{2,1,0:T(8,128)(2,1)} %get-tuple-element.5.turned_ref, bf16[2,128,128]{2,1,0:T(8,128)(2,1)} %get-tuple-element.6.both_ref), custom_call_target="tpu_custom_call" | custom-call | tf_op jit(solution)/shard_map/pallas_call | solution.py:541

commit v5 on v4

--- a/solution.py
+++ b/solution.py
@@ -356,7 +356,7 @@
             a_all[2 * h + u, yl, yh] = (dq[:, u * 128 : (u + 1) * 128].T * SCALE).astype(BF)
         for t in range(3):
             a_send(h, t).start()
-        for n, (layer, chunk) in ((3, (1, 2)),):
+        for n, (layer, chunk) in ((3, (1, 2)), (4, (1, 4))):
             pl.when(h == n)(lambda: poll(layer, chunk))
         pl.when(h == 3)(first_layer)
         return carry
@@ -407,7 +407,6 @@
         return carry
 
     lax.fori_loop(0, z + 1, stage_both, 0)
-    poll(1, 4)
     lax.fori_loop(jnp.maximum(z - 1, 0), z + 1, stage_y, 0)
 
     def finish(layer):

time: 78.1 us -> 77.4 us (level)
  no operation moved by 1% of the time
where the time goes in v5:
time: 77.4 us; the launch traced here: 77.3 us
  Pallas kernels  76.7 us (99%)
    pallas_call x1, Pallas kernels, body(): pl.pallas_call(kernel, out_shape=(jax.ShapeDtypeStruct((2, 640, 128), BF)...  74.8 us
    pallas_call x1, Pallas kernels, body(): pl.pallas_call(outputs_kernel, out_shape=(jax.ShapeDtypeStruct((2, 128, 6...  1.88 us

profile of v5, /device:TPU:1, one launch (start us, length us, event | category | flops | bytes accessed | tf_op | source)
XLA Modules:
  0.0 77.3 jit_solution(18089467362644799152)
XLA Ops:
  0.6 74.8 %shard_map.76 = (bf16[2,640,128]{2,1,0:T(8,128)(2,1)}, bf16[2,128,128]{2,1,0:T(8,128)(2,1)}) custom-call(bf16[2,128,640]{2,1,0:T(8,128)(2,1)} %q_ref.1, bf16[128,128]{1,0:T(8,128)(2,1)} %k_ref.1, bf16[128,128]{1,0:T(8,128)(2,1)} %v_ref.1, bf16[2,128,640]{2,1,0:T(8,128)(2,1)} %do_ref.1, bf16[2,160,640]{2,1,0:T(8,128)(2,1)} %w_ref.1), custom_call_target="tpu_custom_call" | custom-call | tf_op jit(solution)/shard_map/pallas_call | solution.py:505
  75.4 1.9 %shard_map.77 = (bf16[2,128,640]{2,1,0:T(8,128)(2,1)}, bf16[128,128]{1,0:T(8,128)(2,1)}, bf16[128,128]{1,0:T(8,128)(2,1)}) custom-call(bf16[2,640,128]{2,1,0:T(8,128)(2,1)} %get-tuple-element.5.turned_ref, bf16[2,128,128]{2,1,0:T(8,128)(2,1)} %get-tuple-element.6.both_ref), custom_call_target="tpu_custom_call" | custom-call | tf_op jit(solution)/shard_map/pallas_call | solution.py:540

commit v6 on v5

--- a/solution.py
+++ b/solution.py
@@ -431,13 +431,13 @@
     wait_rows(1)
     wait_weights(1, w_all.at[0, :, pl.ds(0, 5), 0])
     second_layer([z, shift(0, 1), shift(1, 1), shift(0, 2), shift(1, 2)])
+    finish(0)
     early = jnp.minimum(z + 1, 2)
     lax.fori_loop(0, early, stage_z, 0)
     poll(1, 5)
     poll(1, 6)
     wait_weights(2, w_all.at[0, :, pl.ds(0, 3), 0])
     second_layer([shift(0, 3), shift(1, 3), shift(0, 4)])
-    finish(0)
 
     middle = jnp.minimum(z + 1, 6)
     lax.fori_loop(early, middle, stage_z, 0)

time: 77.4 us -> 77.4 us (level)
  no operation moved by 1% of the time
where the time goes in v6:
time: 77.4 us; the launch traced here: 77.3 us
  Pallas kernels  76.6 us (99%)
    pallas_call x1, Pallas kernels, body(): pl.pallas_call(kernel, out_shape=(jax.ShapeDtypeStruct((2, 640, 128), BF)...  74.7 us
    pallas_call x1, Pallas kernels, body(): pl.pallas_call(outputs_kernel, out_shape=(jax.ShapeDtypeStruct((2, 128, 6...  1.88 us

profile of v6, /device:TPU:1, one launch (start us, length us, event | category | flops | bytes accessed | tf_op | source)
XLA Modules:
  0.0 77.3 jit_solution(11703549924728074159)
XLA Ops:
  0.6 74.7 %shard_map.76 = (bf16[2,640,128]{2,1,0:T(8,128)(2,1)}, bf16[2,128,128]{2,1,0:T(8,128)(2,1)}) custom-call(bf16[2,128,640]{2,1,0:T(8,128)(2,1)} %q_ref.1, bf16[128,128]{1,0:T(8,128)(2,1)} %k_ref.1, bf16[128,128]{1,0:T(8,128)(2,1)} %v_ref.1, bf16[2,128,640]{2,1,0:T(8,128)(2,1)} %do_ref.1, bf16[2,160,640]{2,1,0:T(8,128)(2,1)} %w_ref.1), custom_call_target="tpu_custom_call" | custom-call | tf_op jit(solution)/shard_map/pallas_call | solution.py:505
  75.4 1.9 %shard_map.77 = (bf16[2,128,640]{2,1,0:T(8,128)(2,1)}, bf16[128,128]{1,0:T(8,128)(2,1)}, bf16[128,128]{1,0:T(8,128)(2,1)}) custom-call(bf16[2,640,128]{2,1,0:T(8,128)(2,1)} %get-tuple-element.5.turned_ref, bf16[2,128,128]{2,1,0:T(8,128)(2,1)} %get-tuple-element.6.both_ref), custom_call_target="tpu_custom_call" | custom-call | tf_op jit(solution)/shard_map/pallas_call | solution.py:540
